TPU v7x, 32 devices: a whole 2x2x4 slice. The times are simulated.
32 devices in a mesh: grp: 2 (over y), view: 8 (over z, x), frame: 2 (over core).
Axes of the slice: x: 2, y: 2, z: 4, core: 2. Of those that a mesh axis runs over, the one named last changes fastest.
Arguments:
- sinogram: float32 [32, 128], P(('grp', 'frame'), 'view'), parts along dimension 0, may hold values from -6 to 6
- stat_weight: float32 [32, 128], P(('grp', 'frame'), 'view'), parts along dimension 0, may hold values from 0.5 to 2
- projector: bfloat16 [128, 230400], P('view'), may hold values from -0.0234375 to 0.0234375
- block_mask: int32 [8, 64], P('view'), may hold values 0 or 1
- kinetic: float32 [2, 460800], P(None, ('grp', 'view', 'frame')), parts along dimension 1, may hold values from 0 to 1
- curvature: float32 [16, 460800], P(None, ('grp', 'view', 'frame')), parts along dimension 1, may hold values from 0.02 to 0.2
- plasma: float32 [7200], P('grp'), parts along dimension 0, may hold values from 0.25 to 8, as said below
- bounds: int32 [34], P('grp'), parts along dimension 0, may hold values from 900 to 3600, as said below
Outputs:
- kinetic_new: float32 [2, 460800], P(None, ('grp', 'view', 'frame')), parts along dimension 1
There are 2 independent parts, one for each index of `grp`. A program takes and returns all parts, laid end to end along the dimension named above; an argument that names none is the same for every part. Nothing has to cross between parts.
Inputs may be any that keep to these rules, and one draw needn't show every extreme that they name: `bounds`: strictly increasing frame boundaries; the first is 900 and the last 3600. Positive plasma activity.
All inputs are finite; a program needn't handle non-finite values. No bound on the sum of `block_mask` on one device may be relied on, other than what follows from the above.
Results may differ from a plain program's by a relative error of at most 0.0038.
Values sent between devices are 32-bit elements; how exact they have to be, the bound alone decides.
A program may use at most 256 MiB of HBM per device.

v0:
```python
import jax
import jax.numpy as jnp
from jax import lax
from jax.sharding import PartitionSpec as P


def frame_tables(bounds, plasma):
    starts = bounds[:-1]
    finish = bounds[1:]
    seconds = jnp.arange(plasma.shape[0], dtype=jnp.int32)
    inside = ((seconds[None, :] >= starts[:, None]) & (seconds[None, :] < finish[:, None])).astype(
        jnp.float32
    )
    reaches = jnp.clip(finish[:, None] - jnp.maximum(seconds[None, :], starts[:, None]), 0).astype(
        jnp.float32
    )
    length = (finish - starts).astype(jnp.float32)
    plasma_mean = jnp.dot(inside, plasma, precision=lax.Precision.HIGHEST) / length
    integral = jnp.dot(reaches, plasma, precision=lax.Precision.HIGHEST) / (
        length * plasma.shape[0]
    )
    return (integral, plasma_mean)


def fit_kinetic(curvature, integral, plasma_mean, rhs_slope, rhs_inter):
    coef_cc = jnp.sum(curvature * (integral * integral)[:, None], axis=0)
    coef_cp = jnp.sum(curvature * (integral * plasma_mean)[:, None], axis=0)
    coef_pp = jnp.sum(curvature * (plasma_mean * plasma_mean)[:, None], axis=0)
    determinant = coef_cc * coef_pp - coef_cp * coef_cp
    slope = (coef_pp * rhs_slope - coef_cp * rhs_inter) / determinant
    intercept = (coef_cc * rhs_inter - coef_cp * rhs_slope) / determinant
    return jnp.stack([slope, intercept])


def local(sinogram, stat_weight, projector, block_mask, kinetic, curvature, plasma, bounds):
    integral, plasma_mean = frame_tables(bounds, plasma)
    frame_rows = sinogram.shape[0]
    first_row = lax.axis_index("frame") * frame_rows
    own_integral = lax.dynamic_slice_in_dim(integral, first_row, frame_rows, 0)
    own_level = lax.dynamic_slice_in_dim(plasma_mean, first_row, frame_rows, 0)
    voxels = projector.shape[1]
    gates = jnp.repeat(block_mask[0].astype(jnp.bfloat16), voxels // block_mask.shape[1])
    portion = lax.all_gather(kinetic, ("view", "frame"), axis=1, tiled=True)
    images = (
        own_integral[:, None] * portion[0][None, :] + own_level[:, None] * portion[1][None, :]
    ).astype(jnp.bfloat16)
    images = images * gates
    projection = lax.dot_general(
        images, projector, (((1,), (1,)), ((), ())), preferred_element_type=jnp.float32
    )
    residual = (stat_weight * (sinogram - projection)).astype(jnp.bfloat16)
    backproj = jnp.dot(residual, projector, preferred_element_type=jnp.float32) * gates[None, :]
    frames_fine = (
        integral[:, None] * kinetic[0][None, :] + plasma_mean[:, None] * kinetic[1][None, :]
    )
    owned = lax.psum_scatter(backproj, "view", scatter_dimension=1, tiled=True)
    gradient = lax.all_to_all(owned, "frame", split_axis=1, concat_axis=0, tiled=True)
    target = frames_fine + gradient / curvature
    rhs_slope = jnp.sum(curvature * integral[:, None] * target, axis=0)
    rhs_inter = jnp.sum(curvature * plasma_mean[:, None] * target, axis=0)
    return fit_kinetic(curvature, integral, plasma_mean, rhs_slope, rhs_inter)


def solution(mesh):
    in_specs = (
        P(("grp", "frame"), "view"),
        P(("grp", "frame"), "view"),
        P("view", None),
        P("view", None),
        P(None, ("grp", "view", "frame")),
        P(None, ("grp", "view", "frame")),
        P("grp"),
        P("grp"),
    )
    out_specs = P(None, ("grp", "view", "frame"))
    return jax.shard_map(local, mesh=mesh, in_specs=in_specs, out_specs=out_specs, check_vma=False)
```

profile of v0, /device:TPU:0, one launch (start us, length us, event | category | flops | bytes accessed | tf_op | source)
XLA Modules:
  0.0 219.2 jit_solution(11106135438726170569)
XLA Ops:
  6.5 0.0 copy-start.2
  6.5 0.0 copy-start.3
  6.5 0.0 all-gather.3.cloned.1.call-start
  6.5 0.7 all-gather.3.cloned.1.call-update
  7.3 0.0 reduce-scatter.2.cloned.1.call-start
  7.3 0.7 reshape.107
  8.0 0.8 fusion.35
  8.9 0.3 fusion.17
  9.2 0.1 dynamic_slice.7
  9.3 0.5 fusion.34
  9.8 0.1 dynamic_slice.6
  9.9 0.7 convert_bitcast_fusion
  10.5 0.1 broadcast_in_dim.2
  10.6 0.7 mul.234
  11.4 0.1 convert_element_type.33
  11.4 41.6 %all-gather.3.cloned.1.call-done = f32[16,14400,2]{1,2,0:T(2,128)} async-done(((f32[1,14400,2]{1,2,0:T(2,128)}), f32[16,14400,2]{1,2,0:T(2,128)}) %all-gather.3.cloned.1.call-update) | async-done | bytes 1843216 | tf_op jit(solution)/shard_map/all_gather | solution.py:43
  53.0 1.6 copy.12
  54.6 3.0 %reshape.106 = f32[230400,2]{0,1:T(2,128)} reshape(f32[16,14400,2]{1,0,2:T(8,128)S(1)} %copy.12) | data formatting | bytes 3686400
  57.6 0.0 slice-start
  57.6 3.6 %fusion.33 = (f32[1,230400]{1,0:T(1,128)S(1)}, f32[1,230400]{1,0:T(1,128)S(1)}) fusion(f32[2,230400]{1,0:T(2,128)} %bitcast.35), kind=kLoop, calls=%fused_computation.44 | loop fusion | bytes 3686400 | tf_op jit(solution)/shard_map/slice | solution.py:45
  61.2 0.0 copy-done.2
  61.3 0.0 copy-done.3
  61.3 0.0 slice-start.1
  61.3 5.7 %fusion.14 = bf16[8,16]{1,0:T(8,128)(2,1)S(1)} fusion(f32[8,16]{1,0:T(8,128)S(1)} %copy-done.2, f32[8,16]{1,0:T(8,128)S(1)} %copy-done.3, bf16[16,230400]{1,0:T(8,128)(2,1)} %param.10, f32[230400]{0:T(1024)S(1)} %bitcast.37, f32[8]{0:T(128)S(1)} %dynamic_slice.7, f32[230400]{0:T(1024)S(1)} %bitcast.36, f32[8]{0:T(128)S(1)} %dynamic_slice.6, ...), kind=kOutput, calls=%fused_computation.11 | convolution fusion | flops 68198784 | bytes 9678144 | tf_op jit(solution)/shard_map/dot_general | solution.py:48
  67.0 0.0 slice-done
  67.0 0.0 slice-done.1
  67.0 4.4 %convolution_multiply_fusion = f32[8,230400]{1,0:T(8,128)} fusion(bf16[8,16]{1,0:T(8,128)(2,1)S(1)} %fusion.14, bf16[16,230400]{1,0:T(8,128)(2,1)S(1)} %bitcast.34, f32[230400]{0:T(1024)S(1)} %convert_element_type.33), kind=kOutput, calls=%fused_computation | convolution fusion | flops 60825600 | bytes 15667456 | tf_op jit(solution)/shard_map/dot_general | solution.py:52
  71.3 0.0 copy-start.1
  71.3 0.0 copy-start
  71.3 0.0 reduce-scatter.2.cloned.1.call-update
  71.4 0.9 copy-done.1
  72.2 0.3 slice_reduce_fusion.1
  72.5 131.4 %reduce-scatter.2.cloned.1.call-done = f32[8,28800]{1,0:T(8,128)} async-done(((f32[8,230400]{1,0:T(8,128)}), f32[8,28800]{1,0:T(8,128)}) %reduce-scatter.2.cloned.1.call-update) | async-done | bytes 921616 | tf_op jit(solution)/shard_map/reduce_scatter | solution.py:56
  204.0 1.9 all_to_all.14
  205.8 0.1 copy.13
  205.9 4.4 %all_to_all.19 = f32[8,2,14400]{2,0,1:T(8,128)S(1)} all-to-all(f32[8,2,14400]{2,0,1:T(8,128)S(1)} %copy.13), channel_id=1, replica_groups=mesh['grp'=2,'view'=8,'frame'=2] {'frame'}, dimensions={1} | all-to-all | bytes 1843200 | tf_op jit(solution)/shard_map/all_to_all | solution.py:57
  210.4 0.0 copy-done
  210.4 1.1 multiply_reduce_fusion.4
  211.6 0.8 pad_maximum_fusion
  (4 shorter events, 0.1 us)
Async XLA Ops:
  6.5 54.7 %copy-start.2 = (f32[8,16]{1,0:T(8,128)S(1)}, f32[8,16]{1,0:T(8,128)}, u32[]{:S(2)}) copy-start(f32[8,16]{1,0:T(8,128)} %param.9) | copy-start | bytes 1540
  6.5 54.7 %copy-start.3 = (f32[8,16]{1,0:T(8,128)S(1)}, f32[8,16]{1,0:T(8,128)}, u32[]{:S(2)}) copy-start(f32[8,16]{1,0:T(8,128)} %param.8) | copy-start | bytes 1540
  6.5 46.4 %all-gather.3.cloned.1.call-start = ((), (), s32[]{:S(2)}) async-start(), calls=%async_computation.3 | async-start | bytes 1967104 | tf_op jit(solution)/shard_map/all_gather | solution.py:43
  7.3 196.7 %reduce-scatter.2.cloned.1.call-start = ((), (), s32[]{:S(2)}) async-start(), calls=%async_computation.2 | async-start | bytes 8294400 | tf_op jit(solution)/shard_map/reduce_scatter | solution.py:56
  57.6 9.3 %slice-start = ((s8[7372800]{0:T(1024)(128)(4,1)}), s8[4194304]{0:T(1024)(128)(4,1)S(1)}, s32[]{:S(2)}) async-start(s8[7372800]{0:T(1024)(128)(4,1)} %bitcast.33), calls=%async_computation.4 | async-start | bytes 8388608
  61.3 5.7 %slice-start.1 = ((s8[7372800]{0:T(1024)(128)(4,1)}), s8[3178496]{0:T(1024)(128)(4,1)S(1)}, s32[]{:S(2)}) async-start(s8[7372800]{0:T(1024)(128)(4,1)} %bitcast.33), calls=%async_computation.5 | async-start | bytes 6356992
  71.3 0.9 copy-start.1
  71.3 139.0 %copy-start = (f32[16,14400]{1,0:T(8,128)S(1)}, f32[16,14400]{1,0:T(8,128)}, u32[]{:S(2)}) copy-start(f32[16,14400]{1,0:T(8,128)} %param.13) | copy-start | bytes 2764804
Sparse Core Ops, SparseCore 0:
  9.6 43.3 all-gather.2
  71.5 132.4 reduce-scatter.1
where the time goes:
time: 220 us; the launch traced here: 219 us
  waiting for transfers between devices  174 us (79%)
  local copies, waits for them, and re-layouts  14 us (6%)
  between operations  13.5 us (6%)
  matrix products  10.8 us (5%)
  blocking collectives  4.44 us (2%)
  other arithmetic  2.62 us (1%)
    reduce_scatter x1, waiting for transfers between devices, local(): owned = lax.psum_scatter(backproj, 'view', scatter_dimension=1, tiled=True)  131 us
    all_gather x1, waiting for transfers between devices, local(): portion = lax.all_gather(kinetic, ('view', 'frame'), axis=1, tiled=True)  41.6 us
    dot_general x1, matrix products, local(): lax.dot_general(images, projector, (((1,), (1,)), ((), ())), preferred_el...  5.68 us
    unnamed x14, local copies, waits for them, and re-layouts  4.63 us
    all_to_all x1, blocking collectives, local(): lax.all_to_all(owned, 'frame', split_axis=1, concat_axis=0, tiled=True)  4.44 us
  transfers between devices with their start and end apart: 2, of which 2 were waited for; matrix products, arithmetic and copies ran while one was open for 2% of the time, Pallas kernels for 0%

commit v1 on v0

v1 whole, which is shorter than its diff:
```python
import jax
import jax.numpy as jnp
from jax import lax
from jax.experimental import pallas as pl
from jax.experimental.pallas import tpu as pltpu
from jax.sharding import PartitionSpec as P


def frame_tables(bounds, plasma):
    starts = bounds[:-1]
    finish = bounds[1:]
    seconds = jnp.arange(plasma.shape[0], dtype=jnp.int32)
    inside = ((seconds[None, :] >= starts[:, None]) & (seconds[None, :] < finish[:, None])).astype(
        jnp.float32
    )
    reaches = jnp.clip(finish[:, None] - jnp.maximum(seconds[None, :], starts[:, None]), 0).astype(
        jnp.float32
    )
    length = (finish - starts).astype(jnp.float32)
    plasma_mean = jnp.sum(inside * plasma[None, :], axis=1) / length
    integral = jnp.sum(reaches * plasma[None, :], axis=1) / (length * plasma.shape[0])
    return (integral, plasma_mean)


def split_rows(rows):
    high = lax.reduce_precision(rows, 8, 7)
    middle = lax.reduce_precision(rows - high, 8, 7)
    low = rows - high - middle
    return jnp.concatenate([high, middle, low], axis=0).astype(jnp.bfloat16)


def solve(curvature, integral, plasma_mean, kinetic, slope_sum, inter_sum):
    coef_cc = jnp.sum(curvature * (integral * integral)[:, None], axis=0)
    coef_cp = jnp.sum(curvature * (integral * plasma_mean)[:, None], axis=0)
    coef_pp = jnp.sum(curvature * (plasma_mean * plasma_mean)[:, None], axis=0)
    determinant = coef_cc * coef_pp - coef_cp * coef_cp
    slope = kinetic[0] + (coef_pp * slope_sum - coef_cp * inter_sum) / determinant
    intercept = kinetic[1] + (coef_cc * inter_sum - coef_cp * slope_sum) / determinant
    return jnp.stack([slope, intercept])


def plain(sinogram, stat_weight, projector, block_mask, kinetic, curvature, plasma, bounds):
    integral, plasma_mean = frame_tables(bounds, plasma)
    frame_rows = sinogram.shape[0]
    first_row = lax.axis_index("frame") * frame_rows
    own_integral = lax.dynamic_slice_in_dim(integral, first_row, frame_rows, 0)
    own_level = lax.dynamic_slice_in_dim(plasma_mean, first_row, frame_rows, 0)
    voxels = projector.shape[1]
    gates = jnp.repeat(block_mask[0].astype(jnp.bfloat16), voxels // block_mask.shape[1])
    portion = lax.all_gather(kinetic, ("view", "frame"), axis=1, tiled=True)
    images = (
        own_integral[:, None] * portion[0][None, :] + own_level[:, None] * portion[1][None, :]
    ).astype(jnp.bfloat16)
    images = images * gates
    projection = lax.dot_general(
        images, projector, (((1,), (1,)), ((), ())), preferred_element_type=jnp.float32
    )
    residual = lax.reduce_precision(stat_weight * (sinogram - projection), 8, 7)
    weighted = jnp.stack(
        [
            jnp.sum(own_integral[:, None] * residual, axis=0),
            jnp.sum(own_level[:, None] * residual, axis=0),
        ]
    )
    parts = jnp.dot(split_rows(weighted), projector, preferred_element_type=jnp.float32)
    partial = (parts[0:2] + parts[2:4] + parts[4:6]) * gates[None, :]
    owned = lax.psum_scatter(partial, ("view", "frame"), scatter_dimension=1, tiled=True)
    return solve(curvature, integral, plasma_mean, kinetic, owned[0], owned[1])


MESH = pl.DeviceIdType.MESH
PIECES = 6


def rounded(values):
    return values.astype(jnp.bfloat16).astype(jnp.float32)


def kernel(
    kinetic_ref, plasma_ref, sinogram_ref, weight_ref, bounds_ref, mask_ref, projector_ref, curvature_ref,
    out_ref,
    kin, mat, curv, coef, counts, proj, xsend, xrecv, zsend, zrecv, lhs,
    mat_sem, curv_sem, ksend_x, ksend_z, ksend_own, krecv, count_sem, proj_sem, xs_sem, xr_sem, zs_sem, zr_sem,
):
    view = lax.axis_index("view")
    core = lax.axis_index("frame")
    z, x = view // 2, view % 2
    inner = (z % 2 + z // 2) % 2
    shard = kinetic_ref.shape[1]
    wide = kin.shape[2]
    piece = wide // PIECES
    pad = wide - shard
    frames = curvature_ref.shape[0]
    bins = projector_ref.shape[0]
    samples = plasma_ref.shape[1]
    blocks = mask_ref.shape[1] // 16
    block = shard // blocks
    near = [z, z + 1 - 2 * (z % 2), 2 - z // 2, 3 - 3 * (z // 2)]

    def there(z_to, x_to):
        return {"view": z_to * 2 + x_to}

    other = {"frame": 1 - core}

    def mat_copy(slot):
        start = pl.multiple_of(slot * (2 * shard) + core * (2 * shard - wide), 128)
        return pltpu.make_async_copy(
            projector_ref.at[:, pl.ds(start, wide)], mat.at[slot], mat_sem.at[slot]
        )

    barrier = pltpu.get_barrier_semaphore()
    pl.semaphore_signal(barrier, inc=1, device_id=there(z, 1 - x), device_id_type=MESH)
    pl.semaphore_signal(barrier, inc=1, device_id=other, device_id_type=MESH)

    @pl.when(z > 0)
    def _():
        pl.semaphore_signal(barrier, inc=1, device_id=there(z - 1, x), device_id_type=MESH)

    @pl.when(z < 3)
    def _():
        pl.semaphore_signal(barrier, inc=1, device_id=there(z + 1, x), device_id_type=MESH)

    blank = jnp.zeros((2, pad), jnp.float32)

    @pl.when(core == 0)
    def _():
        kin[view] = jnp.concatenate([kinetic_ref[...], blank], axis=1)

    @pl.when(core == 1)
    def _():
        kin[view] = jnp.concatenate([blank, kinetic_ref[...]], axis=1)

    counts[core, 0] = sinogram_ref[...]
    counts[core, 1] = weight_ref[...]
    pl.semaphore_wait(barrier, 3 + inner)

    def send_kin(slot, sem, device):
        return pltpu.make_async_remote_copy(
            src_ref=kin.at[slot], dst_ref=kin.at[slot], send_sem=sem, recv_sem=krecv.at[slot],
            device_id=device, device_id_type=MESH,
        )

    @pl.when(z > 0)
    def _():
        send_kin(view, ksend_own.at[0], there(z - 1, x)).start()

    @pl.when(z < 3)
    def _():
        send_kin(view, ksend_own.at[1], there(z + 1, x)).start()

    send_kin(view, ksend_x.at[0], there(z, 1 - x)).start()
    count_copy = pltpu.make_async_remote_copy(
        src_ref=counts.at[core], dst_ref=counts.at[core], send_sem=count_sem.at[0], recv_sem=count_sem.at[1],
        device_id=other, device_id_type=MESH,
    )
    count_copy.start()
    for k in range(4):
        for side in (x, 1 - x):
            mat_copy(near[k] * 2 + side).start()
    curv_copy = pltpu.make_async_copy(curvature_ref, curv, curv_sem)
    curv_copy.start()

    rows = lax.broadcasted_iota(jnp.int32, (frames, 1), 0)
    starts = jnp.zeros((frames, 1), jnp.int32)
    finish = jnp.zeros((frames, 1), jnp.int32)
    for f in range(frames):
        starts = jnp.where(rows == f, bounds_ref[f], starts)
        finish = jnp.where(rows == f, bounds_ref[f + 1], finish)
    seconds = lax.broadcasted_iota(jnp.int32, (frames, samples), 1)
    plasma = plasma_ref[...]
    inside = jnp.where((seconds >= starts) & (seconds < finish), plasma, 0.0)
    reaches = jnp.maximum(finish - jnp.maximum(seconds, starts), 0).astype(jnp.float32) * plasma
    length = (finish - starts).astype(jnp.float32)
    level = jnp.sum(inside, axis=1, keepdims=True) / length
    integral = jnp.sum(reaches, axis=1, keepdims=True) / (length * samples)

    def gate_row(slot, sub):
        first = (slot * 2 + core) * blocks
        lane = lax.broadcasted_iota(jnp.int32, (1, piece), 1) + (sub * piece - core * pad)
        row = jnp.full((1, piece), mask_ref[0, first], jnp.int32)
        for i in range(1, blocks):
            row = jnp.where(lane >= i * block, mask_ref[0, first + i], row)
        return row.astype(jnp.float32)

    def forward(slot, total):
        mat_copy(slot).wait()

        def step(sub, total):
            cols = pl.ds(pl.multiple_of(sub * piece, 128), piece)
            gates = gate_row(slot, sub)
            slope = kin[slot, 0:1, cols] * gates
            inter = kin[slot, 1:2, cols] * gates
            images = (integral * slope + level * inter).astype(jnp.bfloat16)
            return total + lax.dot_general(
                images, mat[slot, :, cols], (((1,), (1,)), ((), ())), preferred_element_type=jnp.float32
            )

        return lax.fori_loop(0, PIECES, step, total)

    total = jnp.zeros((frames, bins), jnp.float32)
    for k in range(4):
        slot = near[k] * 2 + x
        if k > 0:
            onward = 3 - z if k == 1 else 3 * (z // 2)
            send_kin(slot, ksend_x.at[k], there(z, 1 - x)).wait_recv()

            @pl.when(inner == 1)
            def _():
                send_kin(slot, ksend_z.at[k - 1], there(onward, x)).start()

            send_kin(slot, ksend_x.at[k], there(z, 1 - x)).start()
        total = forward(slot, total)
        if k == 0:
            curv_copy.wait()
            for start in range(0, shard, piece):
                size = min(piece, shard - start)
                c = curv[:, start:start + size]
                cc = jnp.sum(c * (integral * integral), axis=0, keepdims=True)
                cp = jnp.sum(c * (integral * level), axis=0, keepdims=True)
                pp = jnp.sum(c * (level * level), axis=0, keepdims=True)
                scale = 1.0 / (cc * pp - cp * cp)
                coef[0:1, start:start + size] = cc * scale
                coef[1:2, start:start + size] = cp * scale
                coef[2:3, start:start + size] = pp * scale
        if k > 0:
            past = near[k - 1] * 2 + (1 - x)
            send_kin(past, ksend_x.at[0], there(z, 1 - x)).wait_recv()
            total = forward(past, total)
    past = near[3] * 2 + (1 - x)
    send_kin(past, ksend_x.at[0], there(z, 1 - x)).wait_recv()
    total = forward(past, total)

    proj[core] = total
    proj_copy = pltpu.make_async_remote_copy(
        src_ref=proj.at[core], dst_ref=proj.at[core], send_sem=proj_sem.at[0], recv_sem=proj_sem.at[1],
        device_id=other, device_id_type=MESH,
    )
    proj_copy.start()
    count_copy.wait()
    proj_copy.wait()
    projection = proj[0] + proj[1]
    sinogram = jnp.concatenate([counts[0, 0], counts[1, 0]], axis=0)
    weight = jnp.concatenate([counts[0, 1], counts[1, 1]], axis=0)
    residual = rounded(weight * (sinogram - projection))
    slope_row = jnp.sum(integral * residual, axis=0, keepdims=True)
    inter_row = jnp.sum(level * residual, axis=0, keepdims=True)
    index = lax.broadcasted_iota(jnp.int32, (16, bins), 0)
    both = jnp.where(index % 2 == 0, slope_row, inter_row)
    high = rounded(both)
    middle = rounded(both - high)
    low = both - high - middle
    lhs[...] = jnp.where(
        index < 2, high, jnp.where(index < 4, middle, jnp.where(index < 6, low, 0.0))
    ).astype(jnp.bfloat16)

    def back(slot, sub):
        cols = pl.ds(pl.multiple_of(sub * piece, 128), piece)
        parts = jnp.dot(lhs[...], mat[slot, :, cols], preferred_element_type=jnp.float32)
        return (parts[0:2] + parts[2:4] + parts[4:6]) * gate_row(slot, sub), cols

    owners = near[::-1]

    def xcopy(k):
        return pltpu.make_async_remote_copy(
            src_ref=xsend.at[k], dst_ref=xrecv.at[k], send_sem=xs_sem.at[k], recv_sem=xr_sem.at[k],
            device_id=there(z, 1 - x), device_id_type=MESH,
        )

    def zcopy(k):
        if k == 2:
            to, place = near[1], 4 + z % 2
        else:
            to = z + 1 - 2 * (z // 2)
            place = owners[0] if k == 0 else (1 - inner) * owners[1] + inner * (4 + z // 2)
        return pltpu.make_async_remote_copy(
            src_ref=zsend.at[k], dst_ref=zrecv.at[place], send_sem=zs_sem.at[k], recv_sem=zr_sem.at[place],
            device_id=there(to, x), device_id_type=MESH,
        )

    def arrived(place):
        pltpu.make_async_remote_copy(
            src_ref=zrecv.at[place], dst_ref=zrecv.at[place], send_sem=zs_sem.at[0], recv_sem=zr_sem.at[place],
            device_id=there(z, 1 - x), device_id_type=MESH,
        ).wait_recv()

    for k in range(4):

        @pl.loop(0, PIECES)
        def _(sub):
            values, cols = back(owners[k] * 2 + 1 - x, sub)
            xsend[k, :, cols] = values

        xcopy(k).start()
    for k in range(4):

        @pl.loop(0, PIECES)
        def _(sub):
            values, cols = back(owners[k] * 2 + x, sub)
            zsend[k, :, cols] = values

    for k in range(4):
        xcopy(k).wait_recv()
        if k < 3:

            @pl.when(inner == 1)
            def _():
                arrived(owners[k])
                zsend[k] = zsend[k] + xrecv[k] + zrecv[owners[k]]

            @pl.when(inner == 0)
            def _():
                zsend[k] = zsend[k] + xrecv[k]

            zcopy(k).start()

    @pl.when(inner == 1)
    def _():
        arrived(4)
        arrived(5)
        zsend[3] = zsend[3] + xrecv[3] + zrecv[4] + zrecv[5]

    @pl.when(inner == 0)
    def _():
        arrived(5 - z // 2)
        zsend[3] = zsend[3] + xrecv[3] + zrecv[5 - z // 2]

    def finish_with(shift):
        slope = zsend[3, 0:1, shift:shift + shard]
        inter = zsend[3, 1:2, shift:shift + shard]
        cc, cp, pp = coef[0:1], coef[1:2], coef[2:3]
        out_ref[0:1] = kinetic_ref[0:1] + (pp * slope - cp * inter)
        out_ref[1:2] = kinetic_ref[1:2] + (cc * inter - cp * slope)

    @pl.when(core == 0)
    def _():
        finish_with(0)

    @pl.when(core == 1)
    def _():
        finish_with(pad)

    for k in range(4):
        xcopy(k).wait_send()
        send_kin(near[k] * 2 + x, ksend_x.at[k], there(z, 1 - x)).wait_send()
    for k in range(3):
        zcopy(k).wait_send()

    @pl.when(inner == 1)
    def _():
        for k in range(1, 4):
            send_kin(near[k] * 2 + x, ksend_z.at[k - 1], there(z, 1 - x)).wait_send()

    @pl.when(z > 0)
    def _():
        send_kin(view, ksend_own.at[0], there(z - 1, x)).wait_send()

    @pl.when(z < 3)
    def _():
        send_kin(view, ksend_own.at[1], there(z + 1, x)).wait_send()


def fused(sinogram, stat_weight, projector, block_mask, kinetic, curvature, plasma, bounds):
    shard = kinetic.shape[1]
    frames = curvature.shape[0]
    bins = projector.shape[0]
    wide = padded_width(shard)
    dma = pltpu.SemaphoreType.DMA
    vmem = pl.BlockSpec(memory_space=pltpu.VMEM)
    smem = pl.BlockSpec(memory_space=pltpu.SMEM)
    hbm = pl.BlockSpec(memory_space=pl.ANY)
    f32 = jnp.float32
    return pl.pallas_call(
        kernel,
        out_shape=jax.ShapeDtypeStruct(kinetic.shape, f32),
        in_specs=[vmem, vmem, vmem, vmem, smem, smem, hbm, hbm],
        out_specs=vmem,
        scratch_shapes=[
            pltpu.VMEM((8, 2, wide), f32),
            pltpu.VMEM((8, bins, wide), jnp.bfloat16),
            pltpu.VMEM((frames, shard), f32),
            pltpu.VMEM((3, shard), f32),
            pltpu.VMEM((2, 2) + sinogram.shape, f32),
            pltpu.VMEM((2, frames, bins), f32),
            pltpu.VMEM((4, 2, wide), f32),
            pltpu.VMEM((4, 2, wide), f32),
            pltpu.VMEM((4, 2, wide), f32),
            pltpu.VMEM((6, 2, wide), f32),
            pltpu.VMEM((16, bins), jnp.bfloat16),
            dma((8,)),
            dma,
            dma((4,)),
            dma((3,)),
            dma((2,)),
            dma((8,)),
            dma((2,)),
            dma((2,)),
            dma((4,)),
            dma((4,)),
            dma((3,)),
            dma((6,)),
        ],
        compiler_params=pltpu.CompilerParams(
            collective_id=0, has_side_effects=True, vmem_limit_bytes=40 * 2**20
        ),
        cost_estimate=pl.CostEstimate(
            flops=2 * frames * projector.size, bytes_accessed=projector.size, transcendentals=0
        ),
    )(kinetic, plasma[None, :], sinogram, stat_weight, bounds, block_mask, projector, curvature)


def padded_width(shard):
    step = 128 * PIECES
    return -(-shard // step) * step


def fits(mesh, projector, block_mask, kinetic, sinogram):
    shard = kinetic.shape[1]
    return (
        mesh.shape["view"] == 8
        and mesh.shape["frame"] == 2
        and 2 * shard % 128 == 0
        and padded_width(shard) <= 2 * shard
        and block_mask.shape[1] % 16 == 0
        and projector.shape == (16, 16 * shard)
        and sinogram.shape == (8, 16)
    )


def solution(mesh):
    in_specs = (
        P(("grp", "frame"), "view"),
        P(("grp", "frame"), "view"),
        P("view", None),
        P("view", None),
        P(None, ("grp", "view", "frame")),
        P(None, ("grp", "view", "frame")),
        P("grp"),
        P("grp"),
    )
    out_specs = P(None, ("grp", "view", "frame"))

    def local(sinogram, stat_weight, projector, block_mask, kinetic, curvature, plasma, bounds):
        form = fused if fits(mesh, projector, block_mask, kinetic, sinogram) else plain
        return form(sinogram, stat_weight, projector, block_mask, kinetic, curvature, plasma, bounds)

    return jax.shard_map(local, mesh=mesh, in_specs=in_specs, out_specs=out_specs, check_vma=False)
```

time: 220 us -> 54.9 us (0.25)
  waiting for transfers between devices: 174 us -> 0 us
  Pallas kernels: 0 us -> 45.3 us
  between operations: 13.5 us -> 0.03 us
  matrix products: 10.8 us -> 0 us
  local copies, waits for them, and re-layouts: 14 us -> 9.23 us
  blocking collectives: 4.44 us -> 0 us
  other arithmetic: 2.62 us -> 0 us
    reduce_scatter x1 -> x0, waiting for transfers between devices: 131 us -> none  [local(): owned = lax.psum_scatter(backproj, 'view', scatter_dimension=1, tiled=True)]
    pallas_call x0 -> x1, Pallas kernels: none -> 45.3 us  [fused(): pl.pallas_call(kernel, out_shape=jax.ShapeDtypeStruct(kinetic.shape, f32)...]
    all_gather x1 -> x0, waiting for transfers between devices: 41.6 us -> none  [local(): portion = lax.all_gather(kinetic, ('view', 'frame'), axis=1, tiled=True)]
    dot_general x4 -> x0, matrix products: 10.8 us -> none  [the longest x1 5.68 us: local(): lax.dot_general(images, projector, (((1,), (1,)), ((), ())), preferred_el...]
    slice x3 -> x0, local copies, waits for them, and re-layouts: 4.72 us -> none  [the longest x1 3.61 us: local(): portion[0][None, :]]
    all_to_all x1 -> x0, blocking collectives: 4.44 us -> none  [local(): lax.all_to_all(owned, 'frame', split_axis=1, concat_axis=0, tiled=True)]
    unnamed x14 -> x15, local copies, waits for them, and re-layouts: 4.63 us -> 8.5 us
  transfers between devices with their start and end apart: 2 -> 0, of which waited for: 2 -> 0; matrix products, arithmetic and copies ran while one was open for 2% -> 0% of each run, Pallas kernels for 0% -> 0%
where the time goes in v1:
time: 54.9 us; the launch traced here: 54.6 us
  Pallas kernels  45.3 us (83%)
  local copies, waits for them, and re-layouts  9.23 us (17%)
    pallas_call x1, Pallas kernels, fused(): pl.pallas_call(kernel, out_shape=jax.ShapeDtypeStruct(kinetic.shape, f32)...  45.3 us
    unnamed x15, local copies, waits for them, and re-layouts  8.5 us

profile of v1, /device:TPU:0, one launch (start us, length us, event | category | flops | bytes accessed | tf_op | source)
XLA Modules:
  0.0 54.6 jit_solution(13993454002858567240)
XLA Ops:
  0.0 0.7 %broadcast_in_dim.3.plasma_ref = f32[1,3600]{1,0:T(1,128)S(1)} reshape(f32[3600]{0:T(1024)} %param.14) | data formatting | bytes 28800 | tf_op jit(solution)/shard_map/broadcast_in_dim | solution.py:408
  0.7 0.0 copy-start
  0.7 3.1 %copy-done = bf16[16,230400]{1,0:T(8,128)(2,1)S(1)} copy-done((bf16[16,230400]{1,0:T(8,128)(2,1)S(1)}, bf16[16,230400]{1,0:T(8,128)(2,1)}, u32[]{:S(2)}) %copy-start) | copy-done | bytes 7372824
  3.8 0.0 copy-start.1
  3.8 1.2 %copy-done.1 = f32[16,14400]{1,0:T(8,128)S(1)} copy-done((f32[16,14400]{1,0:T(8,128)S(1)}, f32[16,14400]{1,0:T(8,128)}, u32[]{:S(2)}) %copy-start.1) | copy-done | bytes 921624
  5.0 0.0 copy-start.2
  5.0 0.9 %copy-done.2 = f32[2,14400]{1,0:T(2,128)S(1)} copy-done((f32[2,14400]{1,0:T(2,128)S(1)}, f32[2,14400]{1,0:T(2,128)}, u32[]{:S(2)}) %copy-start.2) | copy-done | bytes 115224
  5.9 0.0 copy-start.3
  5.9 0.7 %copy-done.3 = f32[8,16]{1,0:T(8,128)S(1)} copy-done((f32[8,16]{1,0:T(8,128)S(1)}, f32[8,16]{1,0:T(8,128)}, u32[]{:S(2)}) %copy-start.3) | copy-done | bytes 536
  6.6 0.0 copy-start.4
  6.6 0.7 %copy-done.4 = f32[8,16]{1,0:T(8,128)S(1)} copy-done((f32[8,16]{1,0:T(8,128)S(1)}, f32[8,16]{1,0:T(8,128)}, u32[]{:S(2)}) %copy-start.4) | copy-done | bytes 536
  7.3 0.0 copy-start.5
  7.3 0.7 %copy-done.5 = s32[17]{0:T(128)S(1)} copy-done((s32[17]{0:T(128)S(1)}, s32[17]{0:T(128)}, u32[]{:S(2)}) %copy-start.5) | copy-done | bytes 92
  7.9 0.0 copy-start.6
  7.9 0.7 %copy-done.6 = s32[1,64]{1,0:T(1,128)S(1)} copy-done((s32[1,64]{1,0:T(1,128)S(1)}, s32[1,64]{1,0:T(1,128)}, u32[]{:S(2)}) %copy-start.6) | copy-done | bytes 280
  8.6 45.3 %shard_map.82 = f32[2,14400]{1,0:T(2,128)S(1)} custom-call(f32[2,14400]{1,0:T(2,128)S(1)} %copy-done.2, f32[1,3600]{1,0:T(1,128)S(1)} %broadcast_in_dim.3.plasma_ref, f32[8,16]{1,0:T(8,128)S(1)} %copy-done.3, f32[8,16]{1,0:T(8,128)S(1)} %copy-done.4, s32[17]{0:T(128)S(1)} %copy-done.5, s32[1,64]{1,0:T(1,128)S(1)} %copy-done.6, ...), custom_call_target="tpu_custom_call" | custom-call | flops 117964800 | bytes 3686400 | tf_op jit(solution)/shard_map/pallas_call | solution.py:372
  53.9 0.6 %copy.10 = f32[2,14400]{1,0:T(2,128)} copy(f32[2,14400]{1,0:T(2,128)S(1)} %shard_map.82) | data formatting | bytes 230400
Async XLA Ops:
  0.7 3.1 %copy-start = (bf16[16,230400]{1,0:T(8,128)(2,1)S(1)}, bf16[16,230400]{1,0:T(8,128)(2,1)}, u32[]{:S(2)}) copy-start(bf16[16,230400]{1,0:T(8,128)(2,1)} %projector_ref.1) | copy-start | bytes 22118404
  3.8 1.2 %copy-start.1 = (f32[16,14400]{1,0:T(8,128)S(1)}, f32[16,14400]{1,0:T(8,128)}, u32[]{:S(2)}) copy-start(f32[16,14400]{1,0:T(8,128)} %curvature_ref.1) | copy-start | bytes 2764804
  5.0 0.9 %copy-start.2 = (f32[2,14400]{1,0:T(2,128)S(1)}, f32[2,14400]{1,0:T(2,128)}, u32[]{:S(2)}) copy-start(f32[2,14400]{1,0:T(2,128)} %kinetic_ref.1) | copy-start | bytes 345604
  5.9 0.7 %copy-start.3 = (f32[8,16]{1,0:T(8,128)S(1)}, f32[8,16]{1,0:T(8,128)}, u32[]{:S(2)}) copy-start(f32[8,16]{1,0:T(8,128)} %sinogram_ref.1) | copy-start | bytes 1540
  6.6 0.7 %copy-start.4 = (f32[8,16]{1,0:T(8,128)S(1)}, f32[8,16]{1,0:T(8,128)}, u32[]{:S(2)}) copy-start(f32[8,16]{1,0:T(8,128)} %weight_ref.1) | copy-start | bytes 1540
  7.3 0.7 %copy-start.5 = (s32[17]{0:T(128)S(1)}, s32[17]{0:T(128)}, u32[]{:S(2)}) copy-start(s32[17]{0:T(128)} %bounds_ref.1) | copy-start | bytes 208
  7.9 0.7 %copy-start.6 = (s32[1,64]{1,0:T(1,128)S(1)}, s32[1,64]{1,0:T(1,128)}, u32[]{:S(2)}) copy-start(s32[1,64]{1,0:T(1,128)} %mask_ref.1) | copy-start | bytes 772

commit v2 on v1

--- a/solution.py
+++ b/solution.py
@@ -70,6 +70,7 @@
 
 MESH = pl.DeviceIdType.MESH
 PIECES = 6
+PARTS = 6
 
 
 def rounded(values):
@@ -77,8 +78,9 @@
 
 
 def kernel(
-    kinetic_ref, plasma_ref, sinogram_ref, weight_ref, bounds_ref, mask_ref, projector_ref, curvature_ref,
+    kinetic_hbm, plasma_hbm, sinogram_hbm, weight_hbm, bounds_hbm, mask_hbm, projector_ref, curvature_ref,
     out_ref,
+    kinetic_ref, plasma_ref, bounds_ref, mask_ref, in_sem,
     kin, mat, curv, coef, counts, proj, xsend, xrecv, zsend, zrecv, lhs,
     mat_sem, curv_sem, ksend_x, ksend_z, ksend_own, krecv, count_sem, proj_sem, xs_sem, xr_sem, zs_sem, zr_sem,
 ):
@@ -89,6 +91,8 @@
     shard = kinetic_ref.shape[1]
     wide = kin.shape[2]
     piece = wide // PIECES
+    span = wide // PARTS
+    each = PIECES // PARTS
     pad = wide - shard
     frames = curvature_ref.shape[0]
     bins = projector_ref.shape[0]
@@ -108,6 +112,21 @@
             projector_ref.at[:, pl.ds(start, wide)], mat.at[slot], mat_sem.at[slot]
         )
 
+    inputs = [
+        pltpu.make_async_copy(source, place, in_sem.at[i])
+        for i, (source, place) in enumerate(
+            [
+                (kinetic_hbm, kinetic_ref),
+                (plasma_hbm, plasma_ref.at[0]),
+                (sinogram_hbm, counts.at[core, 0]),
+                (weight_hbm, counts.at[core, 1]),
+                (bounds_hbm, bounds_ref),
+                (mask_hbm, mask_ref),
+            ]
+        )
+    ]
+    for copy in inputs:
+        copy.start()
     barrier = pltpu.get_barrier_semaphore()
     pl.semaphore_signal(barrier, inc=1, device_id=there(z, 1 - x), device_id_type=MESH)
     pl.semaphore_signal(barrier, inc=1, device_id=other, device_id_type=MESH)
@@ -120,6 +139,7 @@
     def _():
         pl.semaphore_signal(barrier, inc=1, device_id=there(z + 1, x), device_id_type=MESH)
 
+    inputs[0].wait()
     blank = jnp.zeros((2, pad), jnp.float32)
 
     @pl.when(core == 0)
@@ -130,29 +150,37 @@
     def _():
         kin[view] = jnp.concatenate([blank, kinetic_ref[...]], axis=1)
 
-    counts[core, 0] = sinogram_ref[...]
-    counts[core, 1] = weight_ref[...]
     pl.semaphore_wait(barrier, 3 + inner)
 
-    def send_kin(slot, sem, device):
+    def part(q):
+        return pl.ds(pl.multiple_of(q * span, 128), span)
+
+    def send_kin(slot, q, sem, device):
         return pltpu.make_async_remote_copy(
-            src_ref=kin.at[slot], dst_ref=kin.at[slot], send_sem=sem, recv_sem=krecv.at[slot],
-            device_id=device, device_id_type=MESH,
+            src_ref=kin.at[slot, :, part(q)], dst_ref=kin.at[slot, :, part(q)],
+            send_sem=sem, recv_sem=krecv.at[slot, q], device_id=device, device_id_type=MESH,
         )
 
-    @pl.when(z > 0)
-    def _():
-        send_kin(view, ksend_own.at[0], there(z - 1, x)).start()
-
-    @pl.when(z < 3)
-    def _():
-        send_kin(view, ksend_own.at[1], there(z + 1, x)).start()
-
-    send_kin(view, ksend_x.at[0], there(z, 1 - x)).start()
+    across = there(z, 1 - x)
+
+    @pl.loop(0, PARTS)
+    def _(q):
+        @pl.when(z > 0)
+        def _():
+            send_kin(view, q, ksend_own.at[0, q], there(z - 1, x)).start()
+
+        @pl.when(z < 3)
+        def _():
+            send_kin(view, q, ksend_own.at[1, q], there(z + 1, x)).start()
+
+        send_kin(view, q, ksend_x.at[0, q], across).start()
+
     count_copy = pltpu.make_async_remote_copy(
         src_ref=counts.at[core], dst_ref=counts.at[core], send_sem=count_sem.at[0], recv_sem=count_sem.at[1],
         device_id=other, device_id_type=MESH,
     )
+    inputs[2].wait()
+    inputs[3].wait()
     count_copy.start()
     for k in range(4):
         for side in (x, 1 - x):
@@ -160,6 +188,8 @@
     curv_copy = pltpu.make_async_copy(curvature_ref, curv, curv_sem)
     curv_copy.start()
 
+    for i in (1, 4, 5):
+        inputs[i].wait()
     rows = lax.broadcasted_iota(jnp.int32, (frames, 1), 0)
     starts = jnp.zeros((frames, 1), jnp.int32)
     finish = jnp.zeros((frames, 1), jnp.int32)
@@ -182,7 +212,7 @@
             row = jnp.where(lane >= i * block, mask_ref[0, first + i], row)
         return row.astype(jnp.float32)
 
-    def forward(slot, total):
+    def forward(slot, total, landed):
         mat_copy(slot).wait()
 
         def step(sub, total):
@@ -195,40 +225,56 @@
                 images, mat[slot, :, cols], (((1,), (1,)), ((), ())), preferred_element_type=jnp.float32
             )
 
-        return lax.fori_loop(0, PIECES, step, total)
+        for q in range(PARTS):
+            if not landed:
+                send_kin(slot, q, ksend_x.at[0, q], across).wait_recv()
+            total = lax.fori_loop(q * each, (q + 1) * each, step, total)
+        return total
 
     total = jnp.zeros((frames, bins), jnp.float32)
+    total = forward(view, total, True)
+    curv_copy.wait()
+    for start in range(0, shard, piece):
+        size = min(piece, shard - start)
+        c = curv[:, start:start + size]
+        cc = jnp.sum(c * (integral * integral), axis=0, keepdims=True)
+        cp = jnp.sum(c * (integral * level), axis=0, keepdims=True)
+        pp = jnp.sum(c * (level * level), axis=0, keepdims=True)
+        scale = 1.0 / (cc * pp - cp * cp)
+        coef[0:1, start:start + size] = cc * scale
+        coef[1:2, start:start + size] = cp * scale
+        coef[2:3, start:start + size] = pp * scale
+
+    def relay(k, q, onward):
+        slot = near[k] * 2 + x
+        send_kin(slot, q, ksend_x.at[k, q], across).wait_recv()
+        if onward is not None:
+            send_kin(slot, q, ksend_z.at[k - 1, q], there(onward, x)).start()
+        send_kin(slot, q, ksend_x.at[k, q], across).start()
+
+    @pl.when(inner == 0)
+    def _():
+        for k in range(1, 4):
+
+            @pl.loop(0, PARTS)
+            def _(q):
+                relay(k, q, None)
+
+    @pl.when(inner == 1)
+    def _():
+        @pl.loop(0, PARTS)
+        def _(q):
+            relay(1, q, 3 - z)
+            relay(2, q, 3 * (z // 2))
+
+        @pl.loop(0, PARTS)
+        def _(q):
+            relay(3, q, 3 * (z // 2))
+
+    for k in range(1, 4):
+        total = forward(near[k] * 2 + x, total, True)
     for k in range(4):
-        slot = near[k] * 2 + x
-        if k > 0:
-            onward = 3 - z if k == 1 else 3 * (z // 2)
-            send_kin(slot, ksend_x.at[k], there(z, 1 - x)).wait_recv()
-
-            @pl.when(inner == 1)
-            def _():
-                send_kin(slot, ksend_z.at[k - 1], there(onward, x)).start()
-
-            send_kin(slot, ksend_x.at[k], there(z, 1 - x)).start()
-        total = forward(slot, total)
-        if k == 0:
-            curv_copy.wait()
-            for start in range(0, shard, piece):
-                size = min(piece, shard - start)
-                c = curv[:, start:start + size]
-                cc = jnp.sum(c * (integral * integral), axis=0, keepdims=True)
-                cp = jnp.sum(c * (integral * level), axis=0, keepdims=True)
-                pp = jnp.sum(c * (level * level), axis=0, keepdims=True)
-                scale = 1.0 / (cc * pp - cp * cp)
-                coef[0:1, start:start + size] = cc * scale
-                coef[1:2, start:start + size] = cp * scale
-                coef[2:3, start:start + size] = pp * scale
-        if k > 0:
-            past = near[k - 1] * 2 + (1 - x)
-            send_kin(past, ksend_x.at[0], there(z, 1 - x)).wait_recv()
-            total = forward(past, total)
-    past = near[3] * 2 + (1 - x)
-    send_kin(past, ksend_x.at[0], there(z, 1 - x)).wait_recv()
-    total = forward(past, total)
+        total = forward(near[k] * 2 + (1 - x), total, False)
 
     proj[core] = total
     proj_copy = pltpu.make_async_remote_copy(
@@ -260,69 +306,68 @@
 
     owners = near[::-1]
 
-    def xcopy(k):
+    def xcopy(k, q):
         return pltpu.make_async_remote_copy(
-            src_ref=xsend.at[k], dst_ref=xrecv.at[k], send_sem=xs_sem.at[k], recv_sem=xr_sem.at[k],
-            device_id=there(z, 1 - x), device_id_type=MESH,
+            src_ref=xsend.at[k, :, part(q)], dst_ref=xrecv.at[k, :, part(q)],
+            send_sem=xs_sem.at[k, q], recv_sem=xr_sem.at[k, q], device_id=across, device_id_type=MESH,
         )
 
-    def zcopy(k):
+    def zcopy(k, q):
         if k == 2:
             to, place = near[1], 4 + z % 2
         else:
             to = z + 1 - 2 * (z // 2)
             place = owners[0] if k == 0 else (1 - inner) * owners[1] + inner * (4 + z // 2)
         return pltpu.make_async_remote_copy(
-            src_ref=zsend.at[k], dst_ref=zrecv.at[place], send_sem=zs_sem.at[k], recv_sem=zr_sem.at[place],
+            src_ref=zsend.at[k, :, part(q)], dst_ref=zrecv.at[place, :, part(q)],
+            send_sem=zs_sem.at[k, q], recv_sem=zr_sem.at[place, q],
             device_id=there(to, x), device_id_type=MESH,
         )
 
-    def arrived(place):
+    def arrived(place, q):
         pltpu.make_async_remote_copy(
-            src_ref=zrecv.at[place], dst_ref=zrecv.at[place], send_sem=zs_sem.at[0], recv_sem=zr_sem.at[place],
-            device_id=there(z, 1 - x), device_id_type=MESH,
+            src_ref=zrecv.at[place, :, part(q)], dst_ref=zrecv.at[place, :, part(q)],
+            send_sem=zs_sem.at[0, q], recv_sem=zr_sem.at[place, q], device_id=across, device_id_type=MESH,
         ).wait_recv()
 
     for k in range(4):
 
-        @pl.loop(0, PIECES)
-        def _(sub):
-            values, cols = back(owners[k] * 2 + 1 - x, sub)
-            xsend[k, :, cols] = values
-
-        xcopy(k).start()
+        @pl.loop(0, PARTS)
+        def _(q):
+            for i in range(each):
+                values, cols = back(owners[k] * 2 + 1 - x, q * each + i)
+                xsend[k, :, cols] = values
+            xcopy(k, q).start()
+
     for k in range(4):
 
-        @pl.loop(0, PIECES)
-        def _(sub):
-            values, cols = back(owners[k] * 2 + x, sub)
-            zsend[k, :, cols] = values
-
-    for k in range(4):
-        xcopy(k).wait_recv()
-        if k < 3:
+        @pl.loop(0, PARTS)
+        def _(q):
+            for i in range(each):
+                values, cols = back(owners[k] * 2 + x, q * each + i)
+                zsend[k, :, cols] = values
+            cols = part(q)
+            xcopy(k, q).wait_recv()
 
             @pl.when(inner == 1)
             def _():
-                arrived(owners[k])
-                zsend[k] = zsend[k] + xrecv[k] + zrecv[owners[k]]
+                places = (owners[k],) if k < 3 else (4, 5)
+                rest = xrecv[k, :, cols]
+                for place in places:
+                    arrived(place, q)
+                    rest = rest + zrecv[place, :, cols]
+                zsend[k, :, cols] = zsend[k, :, cols] + rest
 
             @pl.when(inner == 0)
             def _():
-                zsend[k] = zsend[k] + xrecv[k]
-
-            zcopy(k).start()
-
-    @pl.when(inner == 1)
-    def _():
-        arrived(4)
-        arrived(5)
-        zsend[3] = zsend[3] + xrecv[3] + zrecv[4] + zrecv[5]
-
-    @pl.when(inner == 0)
-    def _():
-        arrived(5 - z // 2)
-        zsend[3] = zsend[3] + xrecv[3] + zrecv[5 - z // 2]
+                rest = xrecv[k, :, cols]
+                if k == 3:
+                    arrived(5 - z // 2, q)
+                    rest = rest + zrecv[5 - z // 2, :, cols]
+                zsend[k, :, cols] = zsend[k, :, cols] + rest
+
+            if k < 3:
+                zcopy(k, q).start()
 
     def finish_with(shift):
         slope = zsend[3, 0:1, shift:shift + shard]
@@ -339,24 +384,26 @@
     def _():
         finish_with(pad)
 
-    for k in range(4):
-        xcopy(k).wait_send()
-        send_kin(near[k] * 2 + x, ksend_x.at[k], there(z, 1 - x)).wait_send()
-    for k in range(3):
-        zcopy(k).wait_send()
-
-    @pl.when(inner == 1)
-    def _():
-        for k in range(1, 4):
-            send_kin(near[k] * 2 + x, ksend_z.at[k - 1], there(z, 1 - x)).wait_send()
-
-    @pl.when(z > 0)
-    def _():
-        send_kin(view, ksend_own.at[0], there(z - 1, x)).wait_send()
-
-    @pl.when(z < 3)
-    def _():
-        send_kin(view, ksend_own.at[1], there(z + 1, x)).wait_send()
+    @pl.loop(0, PARTS)
+    def _(q):
+        for k in range(4):
+            xcopy(k, q).wait_send()
+            send_kin(near[k] * 2 + x, q, ksend_x.at[k, q], across).wait_send()
+        for k in range(3):
+            zcopy(k, q).wait_send()
+
+        @pl.when(inner == 1)
+        def _():
+            for k in range(1, 4):
+                send_kin(near[k] * 2 + x, q, ksend_z.at[k - 1, q], across).wait_send()
+
+        @pl.when(z > 0)
+        def _():
+            send_kin(view, q, ksend_own.at[0, q], across).wait_send()
+
+        @pl.when(z < 3)
+        def _():
+            send_kin(view, q, ksend_own.at[1, q], across).wait_send()
 
 
 def fused(sinogram, stat_weight, projector, block_mask, kinetic, curvature, plasma, bounds):
@@ -366,15 +413,19 @@
     wide = padded_width(shard)
     dma = pltpu.SemaphoreType.DMA
     vmem = pl.BlockSpec(memory_space=pltpu.VMEM)
-    smem = pl.BlockSpec(memory_space=pltpu.SMEM)
     hbm = pl.BlockSpec(memory_space=pl.ANY)
     f32 = jnp.float32
     return pl.pallas_call(
         kernel,
         out_shape=jax.ShapeDtypeStruct(kinetic.shape, f32),
-        in_specs=[vmem, vmem, vmem, vmem, smem, smem, hbm, hbm],
+        in_specs=[hbm] * 8,
         out_specs=vmem,
         scratch_shapes=[
+            pltpu.VMEM(kinetic.shape, f32),
+            pltpu.VMEM((1,) + plasma.shape, f32),
+            pltpu.SMEM(bounds.shape, jnp.int32),
+            pltpu.SMEM(block_mask.shape, jnp.int32),
+            dma((6,)),
             pltpu.VMEM((8, 2, wide), f32),
             pltpu.VMEM((8, bins, wide), jnp.bfloat16),
             pltpu.VMEM((frames, shard), f32),
@@ -388,24 +439,24 @@
             pltpu.VMEM((16, bins), jnp.bfloat16),
             dma((8,)),
             dma,
-            dma((4,)),
-            dma((3,)),
-            dma((2,)),
-            dma((8,)),
+            dma((4, PARTS)),
+            dma((3, PARTS)),
+            dma((2, PARTS)),
+            dma((8, PARTS)),
             dma((2,)),
             dma((2,)),
-            dma((4,)),
-            dma((4,)),
-            dma((3,)),
-            dma((6,)),
+            dma((4, PARTS)),
+            dma((4, PARTS)),
+            dma((3, PARTS)),
+            dma((6, PARTS)),
         ],
         compiler_params=pltpu.CompilerParams(
-            collective_id=0, has_side_effects=True, vmem_limit_bytes=40 * 2**20
+            collective_id=0, has_side_effects=True, vmem_limit_bytes=56 * 2**20
         ),
         cost_estimate=pl.CostEstimate(
             flops=2 * frames * projector.size, bytes_accessed=projector.size, transcendentals=0
         ),
-    )(kinetic, plasma[None, :], sinogram, stat_weight, bounds, block_mask, projector, curvature)
+    )(kinetic, plasma, sinogram, stat_weight, bounds, block_mask, projector, curvature)
 
 
 def padded_width(shard):

time: 54.9 us -> 38.6 us (0.70)
  Pallas kernels: 45.3 us -> 36.9 us
  local copies, waits for them, and re-layouts: 9.23 us -> 1.55 us
    pallas_call x1, Pallas kernels: 45.3 us -> 36.9 us  [fused(): pl.pallas_call(kernel, out_shape=jax.ShapeDtypeStruct(kinetic.shape, f32)...]
    unnamed x15 -> x1, local copies, waits for them, and re-layouts: 8.5 us -> 1.55 us
    broadcast_in_dim x1 -> x0, local copies, waits for them, and re-layouts: 0.73 us -> none  [fused(): plasma[None, :]]
where the time goes in v2:
time: 38.6 us; the launch traced here: 38.4 us
  Pallas kernels  36.9 us (96%)
  local copies, waits for them, and re-layouts  1.55 us (4%)
    pallas_call x1, Pallas kernels, fused(): pl.pallas_call(kernel, out_shape=jax.ShapeDtypeStruct(kinetic.shape, f32)...  36.9 us
    unnamed x1, local copies, waits for them, and re-layouts  1.55 us

profile of v2, /device:TPU:0, one launch (start us, length us, event | category | flops | bytes accessed | tf_op | source)
XLA Modules:
  0.0 38.4 jit_solution(18332692544891649077)
XLA Ops:
  0.0 36.9 %shard_map.82 = f32[2,14400]{1,0:T(2,128)} custom-call(f32[2,14400]{1,0:T(2,128)} %kinetic_hbm.1, f32[3600]{0:T(1024)} %plasma_hbm.1, f32[8,16]{1,0:T(8,128)} %sinogram_hbm.1, f32[8,16]{1,0:T(8,128)} %weight_hbm.1, s32[17]{0:T(128)} %bounds_hbm.1, s32[1,64]{1,0:T(1,128)} %mask_hbm.1, bf16[16,230400]{1,0:T(8,128)(2,1)} %projector_ref.1, f32[16,14400]{1,0:T(8,128)} %curvature_ref.1), custom_call_target="tpu_custom_call" | custom-call | flops 117964800 | bytes 3686400 | tf_op jit(solution)/shard_map/pallas_call | solution.py:418
  36.9 1.6 %copy.10 = f32[2,14400]{1,0:T(2,128)} copy(f32[2,14400]{1,0:T(2,128)} %shard_map.82) | data formatting | bytes 230400

commit v3 on v2

--- a/solution.py
+++ b/solution.py
@@ -71,6 +71,7 @@
 MESH = pl.DeviceIdType.MESH
 PIECES = 6
 PARTS = 6
+SUM_PARTS = 3
 
 
 def rounded(values):
@@ -306,9 +307,15 @@
 
     owners = near[::-1]
 
+    sum_span = wide // SUM_PARTS
+    sum_each = PIECES // SUM_PARTS
+
+    def sum_part(q):
+        return pl.ds(pl.multiple_of(q * sum_span, 128), sum_span)
+
     def xcopy(k, q):
         return pltpu.make_async_remote_copy(
-            src_ref=xsend.at[k, :, part(q)], dst_ref=xrecv.at[k, :, part(q)],
+            src_ref=xsend.at[k, :, sum_part(q)], dst_ref=xrecv.at[k, :, sum_part(q)],
             send_sem=xs_sem.at[k, q], recv_sem=xr_sem.at[k, q], device_id=across, device_id_type=MESH,
         )
 
@@ -319,34 +326,52 @@
             to = z + 1 - 2 * (z // 2)
             place = owners[0] if k == 0 else (1 - inner) * owners[1] + inner * (4 + z // 2)
         return pltpu.make_async_remote_copy(
-            src_ref=zsend.at[k, :, part(q)], dst_ref=zrecv.at[place, :, part(q)],
+            src_ref=zsend.at[k, :, sum_part(q)], dst_ref=zrecv.at[place, :, sum_part(q)],
             send_sem=zs_sem.at[k, q], recv_sem=zr_sem.at[place, q],
             device_id=there(to, x), device_id_type=MESH,
         )
 
     def arrived(place, q):
         pltpu.make_async_remote_copy(
-            src_ref=zrecv.at[place, :, part(q)], dst_ref=zrecv.at[place, :, part(q)],
+            src_ref=zrecv.at[place, :, sum_part(q)], dst_ref=zrecv.at[place, :, sum_part(q)],
             send_sem=zs_sem.at[0, q], recv_sem=zr_sem.at[place, q], device_id=across, device_id_type=MESH,
         ).wait_recv()
 
     for k in range(4):
 
-        @pl.loop(0, PARTS)
+        @pl.loop(0, SUM_PARTS)
         def _(q):
-            for i in range(each):
-                values, cols = back(owners[k] * 2 + 1 - x, q * each + i)
+            for i in range(sum_each):
+                values, cols = back(owners[k] * 2 + 1 - x, q * sum_each + i)
                 xsend[k, :, cols] = values
             xcopy(k, q).start()
 
+    @pl.loop(0, PARTS)
+    def _(q):
+        for k in range(4):
+            send_kin(near[k] * 2 + x, q, ksend_x.at[k, q], across).wait_send()
+
+        @pl.when(inner == 1)
+        def _():
+            for k in range(1, 4):
+                send_kin(near[k] * 2 + x, q, ksend_z.at[k - 1, q], across).wait_send()
+
+        @pl.when(z > 0)
+        def _():
+            send_kin(view, q, ksend_own.at[0, q], across).wait_send()
+
+        @pl.when(z < 3)
+        def _():
+            send_kin(view, q, ksend_own.at[1, q], across).wait_send()
+
     for k in range(4):
 
-        @pl.loop(0, PARTS)
+        @pl.loop(0, SUM_PARTS)
         def _(q):
-            for i in range(each):
-                values, cols = back(owners[k] * 2 + x, q * each + i)
+            for i in range(sum_each):
+                values, cols = back(owners[k] * 2 + x, q * sum_each + i)
                 zsend[k, :, cols] = values
-            cols = part(q)
+            cols = sum_part(q)
             xcopy(k, q).wait_recv()
 
             @pl.when(inner == 1)
@@ -384,26 +409,12 @@
     def _():
         finish_with(pad)
 
-    @pl.loop(0, PARTS)
+    @pl.loop(0, SUM_PARTS)
     def _(q):
         for k in range(4):
             xcopy(k, q).wait_send()
-            send_kin(near[k] * 2 + x, q, ksend_x.at[k, q], across).wait_send()
         for k in range(3):
             zcopy(k, q).wait_send()
-
-        @pl.when(inner == 1)
-        def _():
-            for k in range(1, 4):
-                send_kin(near[k] * 2 + x, q, ksend_z.at[k - 1, q], across).wait_send()
-
-        @pl.when(z > 0)
-        def _():
-            send_kin(view, q, ksend_own.at[0, q], across).wait_send()
-
-        @pl.when(z < 3)
-        def _():
-            send_kin(view, q, ksend_own.at[1, q], across).wait_send()
 
 
 def fused(sinogram, stat_weight, projector, block_mask, kinetic, curvature, plasma, bounds):
@@ -445,10 +456,10 @@
             dma((8, PARTS)),
             dma((2,)),
             dma((2,)),
-            dma((4, PARTS)),
-            dma((4, PARTS)),
-            dma((3, PARTS)),
-            dma((6, PARTS)),
+            dma((4, SUM_PARTS)),
+            dma((4, SUM_PARTS)),
+            dma((3, SUM_PARTS)),
+            dma((6, SUM_PARTS)),
         ],
         compiler_params=pltpu.CompilerParams(
             collective_id=0, has_side_effects=True, vmem_limit_bytes=56 * 2**20

time: 38.6 us -> 37.6 us (0.974)
  Pallas kernels: 36.9 us -> 35.9 us
    pallas_call x1, Pallas kernels: 36.9 us -> 35.9 us  [fused(): pl.pallas_call(kernel, out_shape=jax.ShapeDtypeStruct(kinetic.shape, f32)...]
where the time goes in v3:
time: 37.6 us; the launch traced here: 37.4 us
  Pallas kernels  35.9 us (95%)
  local copies, waits for them, and re-layouts  1.55 us (4%)
    pallas_call x1, Pallas kernels, fused(): pl.pallas_call(kernel, out_shape=jax.ShapeDtypeStruct(kinetic.shape, f32)...  35.9 us
    unnamed x1, local copies, waits for them, and re-layouts  1.55 us

profile of v3, /device:TPU:0, one launch (start us, length us, event | category | flops | bytes accessed | tf_op | source)
XLA Modules:
  0.0 37.4 jit_solution(12549637666772968560)
XLA Ops:
  0.0 35.9 %shard_map.82 = f32[2,14400]{1,0:T(2,128)} custom-call(f32[2,14400]{1,0:T(2,128)} %kinetic_hbm.1, f32[3600]{0:T(1024)} %plasma_hbm.1, f32[8,16]{1,0:T(8,128)} %sinogram_hbm.1, f32[8,16]{1,0:T(8,128)} %weight_hbm.1, s32[17]{0:T(128)} %bounds_hbm.1, s32[1,64]{1,0:T(1,128)} %mask_hbm.1, bf16[16,230400]{1,0:T(8,128)(2,1)} %projector_ref.1, f32[16,14400]{1,0:T(8,128)} %curvature_ref.1), custom_call_target="tpu_custom_call" | custom-call | flops 117964800 | bytes 3686400 | tf_op jit(solution)/shard_map/pallas_call | solution.py:429
  35.9 1.6 %copy.10 = f32[2,14400]{1,0:T(2,128)} copy(f32[2,14400]{1,0:T(2,128)} %shard_map.82) | data formatting | bytes 230400
